TPU v7x, 512 devices: a whole 4x4x16 slice. The times are simulated.
512 devices in a mesh: chan: 128 (over z, x, core), blk: 4 (over y).
Axes of the slice: x: 4, y: 4, z: 16, core: 2. Of those that a mesh axis runs over, the one named last changes fastest.
Arguments:
- omega: float32 [128, 576, 576], P('chan', 'blk'), may hold values from -0.25 to 0.25
- hamiltonian: float32 [128, 576, 576], P('chan', 'blk'), may hold values from -6 to 6
- pair_occ: float32 [128, 576], P('chan'), may hold values from -1 to 1
- cross_occ: float32 [128, 576], P('chan'), may hold values from -1 to 1
- block_size: int32 [128], P('chan'), may hold values from 288 to 576
- jlabel: int32 [128], replicated, may hold values from 0 to 127
- family: int32 [128], replicated, may hold values from 0 to 3
- sixj: float32 [128, 128], replicated, may hold values from -1 to 1
- column_map: int32 [576], replicated, may hold values from 0 to 575, each once
Outputs:
- evolved: float32 [128, 576, 576], P('chan', 'blk')
Inputs may be any that keep to these rules, and one draw needn't show every extreme that they name: `column_map`: a permutation of 0 to 575.
All inputs are finite; a program needn't handle non-finite values.
Results may differ from a plain program's by a relative error of at most 0.0032.
Values may be sent and summed in bfloat16 or wider, within the bound.
A program may use at most 64 MiB of HBM per device.

v0:
```python
import jax
import jax.numpy as jnp
from jax import lax
from jax.sharding import PartitionSpec as P

exact_mode = lax.Precision.HIGHEST


def in_order(parts, dim):
    parts = jnp.moveaxis(parts, 0, dim)
    lengths = parts.shape
    return parts.reshape(*lengths[:dim], lengths[dim] * lengths[dim + 1], *lengths[dim + 2 :])


def copy_for_each(shard, axis):
    copies = jnp.broadcast_to(shard, (lax.axis_size(axis), *shard.shape))
    return lax.all_to_all(copies, axis, split_axis=0, concat_axis=0, tiled=True)


def gather_directly(shard, axis, dim):
    return in_order(copy_for_each(shard, axis), dim)


def mixing_matrix(jlabel, family, sixj):
    levels = sixj.shape[0]
    one_hot = (jlabel[:, None] == jnp.arange(levels, dtype=jnp.int32)[None, :]).astype(jnp.float32)
    picked = jnp.dot(one_hot, sixj, precision=exact_mode, preferred_element_type=jnp.float32)
    picked = jnp.dot(picked, one_hot.T, precision=exact_mode, preferred_element_type=jnp.float32)
    kindred = (family[:, None] == family[None, :]).astype(jnp.float32)
    return picked * kindred


def commutator(left_rows, left_full, right_rows, weights):
    scaled_left = (left_rows * weights[:, None, :]).astype(jnp.bfloat16)
    scaled_right = (right_rows * weights[:, None, :]).astype(jnp.bfloat16)
    initial = -jnp.einsum(
        "crk,ckq->crq", scaled_right, left_full, preferred_element_type=jnp.float32
    )
    return initial + jnp.einsum(
        "crk,ckq->crq",
        scaled_left,
        lax.all_gather(right_rows.astype(jnp.bfloat16), "blk", axis=1, tiled=True),
        preferred_element_type=jnp.float32,
    )


def through_mixing(stacked, apply_fn):
    chan_size = lax.axis_size("chan")
    members, channels_here, rows_here, block_width = stacked.shape
    shaped = stacked.reshape(
        members, channels_here, chan_size, rows_here * block_width // chan_size
    )
    returned = lax.all_to_all(
        apply_fn(lax.all_to_all(shaped, "chan", split_axis=2, concat_axis=1, tiled=True)),
        "chan",
        split_axis=1,
        concat_axis=2,
        tiled=True,
    )
    return returned.reshape(returned.shape[0], channels_here, rows_here, block_width)


def on_device(
    omega, hamiltonian, pair_occ, cross_occ, block_size, jlabel, family, sixj, column_map
):
    channels_here, rows_here, block_width = omega.shape
    mixing = mixing_matrix(jlabel, family, sixj)
    row_index = lax.axis_index("blk") * rows_here + jnp.arange(rows_here, dtype=jnp.int32)
    col_index = jnp.arange(block_width, dtype=jnp.int32)
    inside_block = (row_index[None, :, None] < block_size[:, None, None]) & (
        col_index[None, None, :] < block_size[:, None, None]
    )
    window_mask = inside_block.astype(jnp.float32)
    generator = omega * window_mask
    start_ham = hamiltonian * window_mask
    inverse_map = jnp.argsort(column_map)

    def forward_mix(received):
        return jnp.einsum(
            "kc,scil->skil",
            mixing,
            received,
            precision=exact_mode,
            preferred_element_type=jnp.float32,
        )

    def reverse_mix(received):
        return jnp.einsum(
            "ck,scil->skil",
            mixing,
            received,
            precision=exact_mode,
            preferred_element_type=jnp.float32,
        )

    crossed = through_mixing(
        jnp.stack([generator[:, :, column_map], start_ham[:, :, column_map]]), forward_mix
    )
    gen_cross = crossed[0]
    ham_cross = crossed[1]
    gen_full = lax.all_gather(generator.astype(jnp.bfloat16), "blk", axis=1, tiled=True)
    first_pp = commutator(generator, gen_full, start_ham, pair_occ)
    cross_full = gather_directly(gen_cross.astype(jnp.bfloat16), "blk", 1)
    first_cc = commutator(gen_cross, cross_full, ham_cross, cross_occ)

    def both_mix(received):
        restored = jnp.einsum(
            "ck,cil->kil",
            mixing,
            received[1],
            precision=exact_mode,
            preferred_element_type=jnp.float32,
        )
        combined = jnp.einsum(
            "kc,cil->kil",
            mixing,
            received[0] + restored,
            precision=exact_mode,
            preferred_element_type=jnp.float32,
        )
        return jnp.stack([restored, combined])

    outcome = through_mixing(jnp.stack([first_pp[:, :, column_map], first_cc]), both_mix)
    eta = first_pp + outcome[0][:, :, inverse_map]
    eta_cross = outcome[1]
    second_pp = commutator(generator, gen_full, eta, pair_occ)
    second_cc = commutator(gen_cross, cross_full, eta_cross, cross_occ)
    second_back = through_mixing(second_cc[None], reverse_mix)[0]
    second = second_pp + second_back[:, :, inverse_map]
    return (start_ham + eta + 0.5 * second) * window_mask


def solution(mesh):
    in_specs = (
        P("chan", "blk", None),
        P("chan", "blk", None),
        P("chan", None),
        P("chan", None),
        P("chan"),
        P(),
        P(),
        P(),
        P(),
    )
    out_specs = P("chan", "blk", None)
    return jax.shard_map(
        on_device, mesh=mesh, in_specs=in_specs, out_specs=out_specs, check_vma=False
    )
```

profile of v0, /device:TPU:33, one launch (start us, length us, event | category | flops | bytes accessed | tf_op | source)
XLA Modules:
  0.0 370.8 jit_solution(17199406350710039180)
XLA Ops:
  0.8 1.2 fusion.21
  2.2 2.2 gather_fusion.1
  5.2 2.2 gather_fusion.2
  8.1 1.5 copy.68
  9.6 19.4 %all-to-all-start = ((f32[2,1,128,648]{3,0,1,2:T(2,128)}), f32[2,1,128,648]{3,0,1,2:T(2,128)S(1)}, u32[]{:S(2)}, u32[]{:S(2)}) async-start(f32[2,1,128,648]{3,0,1,2:T(2,128)} %copy.68), calls=%async_computation | async-start | bytes 1572864 | tf_op jit(solution)/shard_map/all_to_all | solution.py:54
  29.6 44.0 %all-to-all-done = f32[2,1,128,648]{3,0,1,2:T(2,128)S(1)} async-done(((f32[2,1,128,648]{3,0,1,2:T(2,128)}), f32[2,1,128,648]{3,0,1,2:T(2,128)S(1)}, u32[]{:S(2)}, u32[]{:S(2)}) %all-to-all-start) | async-done | bytes 663584 | tf_op jit(solution)/shard_map/all_to_all | solution.py:54
  74.2 0.7 convolution_bitcast_fusion
  74.9 1.3 copy.70
  76.2 6.8 %all-to-all-start.1 = ((f32[2,128,1,648]{3,0,2,1:T(2,128)}), f32[2,128,1,648]{3,0,2,1:T(2,128)}, u32[]{:S(2)}, u32[]{:S(2)}) async-start(f32[2,128,1,648]{3,0,2,1:T(2,128)} %copy.70), calls=%async_computation.1 | async-start | bytes 1572864 | tf_op jit(solution)/shard_map/all_to_all | solution.py:53
  85.1 12.4 %all_gather.15 = bf16[1,576,576]{2,1,0:T(8,128)(2,1)S(1)} all-gather(bf16[1,144,576]{2,1,0:T(8,128)(2,1)S(1)} %get-tuple-element.17), channel_id=1, replica_groups=mesh['chan'=128,'blk'=4] {'blk'}, dimensions={1}, use_global_device_ids=true | all-gather | bytes 829440 | tf_op jit(solution)/shard_map/all_gather | solution.py:101
  97.5 12.1 %all_gather.16 = bf16[1,576,576]{2,1,0:T(8,128)(2,1)S(1)} all-gather(bf16[1,144,576]{2,1,0:T(8,128)(2,1)S(1)} %get-tuple-element.18), channel_id=1, replica_groups=mesh['chan'=128,'blk'=4] {'blk'}, dimensions={1}, use_global_device_ids=true | all-gather | bytes 829440 | tf_op jit(solution)/shard_map/all_gather | solution.py:42
  110.6 2.2 gather_fusion
  113.0 1.1 stack.27
  114.1 13.2 %all-to-all-done.1 = f32[2,128,1,648]{3,0,2,1:T(2,128)} async-done(((f32[2,128,1,648]{3,0,2,1:T(2,128)}), f32[2,128,1,648]{3,0,2,1:T(2,128)}, u32[]{:S(2)}, u32[]{:S(2)}) %all-to-all-start.1) | async-done | bytes 663584 | tf_op jit(solution)/shard_map/all_to_all | solution.py:53
  127.4 2.0 fusion.44
  129.4 1.1 convert_element_type.104
  130.5 0.7 copy.97
  131.3 1.4 convert_element_type.100
  132.7 1.1 convert_element_type.98
  134.2 1.0 broadcast_in_dim.7
  135.2 4.3 %all-to-all-start.2 = ((bf16[4,1,144,576]{3,2,1,0:T(8,128)(2,1)}), bf16[4,1,144,576]{3,2,1,0:T(8,128)(2,1)S(1)}, u32[]{:S(2)}, u32[]{:S(2)}) async-start(bf16[4,1,144,576]{3,2,1,0:T(8,128)(2,1)} %broadcast_in_dim.7), calls=%async_computation.2 | async-start | bytes 1474560 | tf_op jit(solution)/shard_map/all_to_all | solution.py:17
  139.5 18.4 %all_gather.17 = bf16[1,576,576]{2,1,0:T(8,128)(2,1)S(1)} all-gather(bf16[1,144,576]{2,1,0:T(8,128)(2,1)S(1)} %copy-done.12), channel_id=1, replica_groups=mesh['chan'=128,'blk'=4] {'blk'}, dimensions={1}, use_global_device_ids=true | all-gather | bytes 829440 | tf_op jit(solution)/shard_map/all_gather | solution.py:42
  158.8 1.1 fusion.1
  159.9 1.4 stack.31
  161.4 0.8 copy.73
  162.2 53.6 %all_to_all.28 = f32[2,1,128,648]{3,1,0,2:T(1,128)S(1)} all-to-all(f32[2,1,128,648]{3,1,0,2:T(1,128)S(1)} %copy.73), channel_id=1, replica_groups=mesh['chan'=128,'blk'=4] {'chan'}, dimensions={2} | all-to-all | bytes 1327104 | tf_op jit(solution)/shard_map/all_to_all | solution.py:54
  216.4 1.0 copy.88
  218.0 0.7 fusion.19
  219.0 0.7 convolution_bitcast_fusion.2
  219.7 0.9 pad_maximum_fusion.2
  220.6 2.3 copy.76
  222.9 50.7 %all_to_all.29 = f32[2,128,1,648]{3,2,0,1:T(1,128)S(1)} all-to-all(f32[2,128,1,648]{3,2,0,1:T(1,128)S(1)} %copy.76), channel_id=1, replica_groups=mesh['chan'=128,'blk'=4] {'chan'}, dimensions={1} | all-to-all | bytes 1327104 | tf_op jit(solution)/shard_map/all_to_all | solution.py:53
  273.6 1.3 fusion.42
  275.0 1.1 convert_element_type.109
  276.6 11.6 %all_gather.19 = bf16[1,576,576]{2,1,0:T(8,128)(2,1)S(1)} all-gather(bf16[1,144,576]{2,1,0:T(8,128)(2,1)S(1)} %convert_element_type.111), channel_id=1, replica_groups=mesh['chan'=128,'blk'=4] {'blk'}, dimensions={1}, use_global_device_ids=true | all-gather | bytes 829440 | tf_op jit(solution)/shard_map/all_gather | solution.py:42
  289.5 0.7 reshape_broadcast_in_dim.4
  290.2 36.9 %all_to_all.30 = f32[1,1,128,648]{3,1,0,2:T(1,128)S(1)} all-to-all(f32[1,1,128,648]{3,1,0,2:T(1,128)S(1)} %reshape_broadcast_in_dim.4), channel_id=1, replica_groups=mesh['chan'=128,'blk'=4] {'chan'}, dimensions={2} | all-to-all | bytes 663552 | tf_op jit(solution)/shard_map/all_to_all | solution.py:54
  328.4 1.2 copy.82
  329.6 6.2 %all-to-all-start.6 = ((f32[1,128,1,648]{3,2,0,1:T(1,128)}), f32[1,128,1,648]{3,2,0,1:T(1,128)S(1)}, u32[]{:S(2)}, u32[]{:S(2)}) async-start(f32[1,128,1,648]{3,2,0,1:T(1,128)} %copy.82), calls=%async_computation.6 | async-start | bytes 786432 | tf_op jit(solution)/shard_map/all_to_all | solution.py:53
  336.5 4.4 %sort.17 = (s32[576]{0:T(1024)}, s32[576]{0:T(1024)S(1)}) sort(s32[576]{0:T(1024)S(1)} %copy-done.18, s32[576]{0:T(1024)S(1)} %iota.20), dimensions={0}, to_apply=%region_0.0 | sort | flops 5760 | bytes 9216 | tf_op jit(solution)/shard_map/jit(argsort)/sort | solution.py:76
  341.5 2.2 gather_fusion.3
  344.0 11.7 %all-gather = bf16[576,576]{1,0:T(8,128)(2,1)S(1)} all-gather(bf16[144,576]{1,0:T(8,128)(2,1)S(1)} %fusion.33), channel_id=2, replica_groups=mesh['chan'=128,'blk'=4] {'blk'}, dimensions={0}, use_global_device_ids=true | all-gather | bytes 829440 | tf_op jit(solution)/shard_map/all_gather | solution.py:42
  355.6 1.2 fusion.39
  356.8 7.2 %all-to-all-done.6 = f32[1,128,1,648]{3,2,0,1:T(1,128)S(1)} async-done(((f32[1,128,1,648]{3,2,0,1:T(1,128)}), f32[1,128,1,648]{3,2,0,1:T(1,128)S(1)}, u32[]{:S(2)}, u32[]{:S(2)}) %all-to-all-start.6) | async-done | bytes 331808 | tf_op jit(solution)/shard_map/all_to_all | solution.py:53
  364.0 0.9 reduce.3
  365.6 2.8 gather_fusion.4
  368.4 1.3 copy.84
  369.7 1.1 fusion.8
  (93 shorter events, 14.1 us)
Async XLA Ops:
  0.0 29.0 %copy-start = (f32[128,128]{1,0:T(8,128)S(1)}, f32[128,128]{1,0:T(8,128)}, u32[]{:S(2)}) copy-start(f32[128,128]{1,0:T(8,128)} %param.16) | copy-start | bytes 196612
  0.0 0.7 copy-start.17
  0.7 109.2 %copy-start.13 = (pred[576]{0:T(1024)(128)(4,1)}, pred[576]{0:T(1024)(128)(4,1)S(1)}, u32[]{:S(2)}) copy-start(pred[576]{0:T(1024)(128)(4,1)S(1)} %iota_compare_fusion.3) | copy-start | bytes 1732
  0.8 109.2 %copy-start.15 = (pred[144]{0:T(512)(128)(4,1)}, pred[144]{0:T(512)(128)(4,1)S(1)}, u32[]{:S(2)}) copy-start(pred[144]{0:T(512)(128)(4,1)S(1)} %add_compare_fusion) | copy-start | bytes 436
  9.6 19.5 %copy-start.21 = (s32[128]{0:T(128)S(1)}, s32[128]{0:T(128)}, u32[]{:S(2)}) copy-start(s32[128]{0:T(128)} %param.14) | copy-start | bytes 1540
  9.6 19.7 %copy-start.22 = (s32[128]{0:T(128)S(1)}, s32[128]{0:T(128)}, u32[]{:S(2)}) copy-start(s32[128]{0:T(128)} %param.15) | copy-start | bytes 1540
  9.6 64.0 %all-to-all-start = ((f32[2,1,128,648]{3,0,1,2:T(2,128)}), f32[2,1,128,648]{3,0,1,2:T(2,128)S(1)}, u32[]{:S(2)}, u32[]{:S(2)}) async-start(f32[2,1,128,648]{3,0,1,2:T(2,128)} %copy.68), calls=%async_computation | async-start | bytes 1572864 | tf_op jit(solution)/shard_map/all_to_all | solution.py:54
  76.2 6.9 %copy-start.19 = (f32[1,576]{1,0:T(1,128)S(1)}, f32[1,576]{1,0:T(1,128)}, u32[]{:S(2)}) copy-start(f32[1,576]{1,0:T(1,128)} %param.11) | copy-start | bytes 6916
  76.2 51.1 %all-to-all-start.1 = ((f32[2,128,1,648]{3,0,2,1:T(2,128)}), f32[2,128,1,648]{3,0,2,1:T(2,128)}, u32[]{:S(2)}, u32[]{:S(2)}) async-start(f32[2,128,1,648]{3,0,2,1:T(2,128)} %copy.70), calls=%async_computation.1 | async-start | bytes 1572864 | tf_op jit(solution)/shard_map/all_to_all | solution.py:53
  83.1 0.7 copy-start.20
  83.8 1.0 copy-start.1
  83.8 1.1 copy-start.2
  84.9 46.3 %copy-start.3 = (f32[1,128,1,648]{3,1,2,0:T(8,128)}, f32[1,128,1,648]{3,1,2,0:T(8,128)S(1)}, u32[]{:S(2)}) copy-start(f32[1,128,1,648]{3,1,2,0:T(8,128)S(1)} %mul.105) | copy-start | bytes 995332
  134.2 23.7 %copy-start.5 = (bf16[144,576]{1,0:T(8,128)(2,1)}, bf16[144,576]{1,0:T(8,128)(2,1)S(1)}, u32[]{:S(2)}) copy-start(bf16[144,576]{1,0:T(8,128)(2,1)S(1)} %convert_element_type.102) | copy-start | bytes 497668
  135.2 4.3 %copy-start.12 = (bf16[1,144,576]{2,1,0:T(8,128)(2,1)S(1)}, bf16[1,144,576]{2,1,0:T(8,128)(2,1)}, u32[]{:S(2)}) copy-start(bf16[1,144,576]{2,1,0:T(8,128)(2,1)} %convert_element_type.104) | copy-start | bytes 497668
  135.2 23.0 %all-to-all-start.2 = ((bf16[4,1,144,576]{3,2,1,0:T(8,128)(2,1)}), bf16[4,1,144,576]{3,2,1,0:T(8,128)(2,1)S(1)}, u32[]{:S(2)}, u32[]{:S(2)}) async-start(bf16[4,1,144,576]{3,2,1,0:T(8,128)(2,1)} %broadcast_in_dim.7), calls=%async_computation.2 | async-start | bytes 1474560 | tf_op jit(solution)/shard_map/all_to_all | solution.py:17
  157.9 0.9 copy-start.10
  159.9 1.4 copy-start.7
  218.0 1.0 copy-start.9
  273.6 1.3 copy-start.4
  276.6 11.6 %copy-start.6 = (bf16[144,576]{1,0:T(8,128)(2,1)S(1)}, bf16[144,576]{1,0:T(8,128)(2,1)}, u32[]{:S(2)}) copy-start(bf16[144,576]{1,0:T(8,128)(2,1)} %copy-done.5) | copy-start | bytes 497668
  288.2 0.9 copy-start.11
  329.6 34.4 %all-to-all-start.6 = ((f32[1,128,1,648]{3,2,0,1:T(1,128)}), f32[1,128,1,648]{3,2,0,1:T(1,128)S(1)}, u32[]{:S(2)}, u32[]{:S(2)}) async-start(f32[1,128,1,648]{3,2,0,1:T(1,128)} %copy.82), calls=%async_computation.6 | async-start | bytes 786432 | tf_op jit(solution)/shard_map/all_to_all | solution.py:53
  335.8 0.7 copy-start.18
  343.9 11.7 %copy-start.14 = (pred[576]{0:T(1024)(128)(4,1)S(1)}, pred[576]{0:T(1024)(128)(4,1)}, u32[]{:S(2)}) copy-start(pred[576]{0:T(1024)(128)(4,1)} %copy-done.13) | copy-start | bytes 1732
  343.9 11.7 %copy-start.16 = (pred[144]{0:T(512)(128)(4,1)S(1)}, pred[144]{0:T(512)(128)(4,1)}, u32[]{:S(2)}) copy-start(pred[144]{0:T(512)(128)(4,1)} %copy-done.15) | copy-start | bytes 436
  368.4 1.3 copy-start.8
where the time goes:
time: 372 us; the launch traced here: 371 us
  blocking collectives  207 us (56%)
  waiting for transfers between devices  64.5 us (17%)
  local copies, waits for them, and re-layouts  44.6 us (12%)
  starting transfers between devices  36.8 us (10%)
  matrix products  8.37 us (2%)
  other arithmetic  7.91 us (2%)
    all_to_all x2, blocking collectives, through_mixing(): lax.all_to_all(shaped, 'chan', split_axis=2, concat_axis=1, tiled=True)  90.5 us
    all_gather x4, blocking collectives, commutator(): lax.all_gather(right_rows.astype(jnp.bfloat16), 'blk', axis=1, tiled=True)  53.7 us
    all_to_all x1, blocking collectives, through_mixing(): lax.all_to_all(apply_fn(lax.all_to_all(shaped, 'chan', split_axis=2, conc...  50.7 us
    all_to_all x1, waiting for transfers between devices, through_mixing(): lax.all_to_all(shaped, 'chan', split_axis=2, concat_axis=1, tiled=True)  44 us
    all_to_all x2, waiting for transfers between devices, through_mixing(): lax.all_to_all(apply_fn(lax.all_to_all(shaped, 'chan', split_axis=2, conc...  20.4 us
    all_to_all x1, starting transfers between devices, through_mixing(): lax.all_to_all(shaped, 'chan', split_axis=2, concat_axis=1, tiled=True)  19.4 us
    all_to_all x2, starting transfers between devices, through_mixing(): lax.all_to_all(apply_fn(lax.all_to_all(shaped, 'chan', split_axis=2, conc...  13 us
    all_gather x1, blocking collectives, on_device(): lax.all_gather(generator.astype(jnp.bfloat16), 'blk', axis=1, tiled=True)  12.4 us
  transfers between devices with their start and end apart: 4, of which 3 were waited for; matrix products, arithmetic and copies ran while one was open for 4% of the time, Pallas kernels for 0%

commit v1 on v0

--- a/solution.py
+++ b/solution.py
@@ -1,9 +1,20 @@
+import functools
 import jax
 import jax.numpy as jnp
 from jax import lax
 from jax.sharding import PartitionSpec as P
 
 exact_mode = lax.Precision.HIGHEST
+
+
+def search_the_spans(slab_in, mesh_ax):
+    w_next = jnp.stack([slab_in for _ in range(lax.psum(1, axis_name=mesh_ax))])
+    response = lax.all_to_all(w_next, axis_name=mesh_ax, split_axis=0, concat_axis=0)
+    now = jnp.concatenate(response, axis=1)
+    return now
+
+
+remake_space_by_axis = functools.partial(search_the_spans, mesh_ax="blk")
 
 
 def in_order(parts, dim):
@@ -98,7 +109,7 @@
     )
     gen_cross = crossed[0]
     ham_cross = crossed[1]
-    gen_full = lax.all_gather(generator.astype(jnp.bfloat16), "blk", axis=1, tiled=True)
+    gen_full = remake_space_by_axis(generator.astype(jnp.bfloat16))
     first_pp = commutator(generator, gen_full, start_ham, pair_occ)
     cross_full = gather_directly(gen_cross.astype(jnp.bfloat16), "blk", 1)
     first_cc = commutator(gen_cross, cross_full, ham_cross, cross_occ)

time: 372 us -> 386 us (1.038)
  waiting for transfers between devices: 64.5 us -> 85.6 us
  blocking collectives: 207 us -> 195 us
  starting transfers between devices: 36.8 us -> 40.9 us
    all_to_all x2, waiting for transfers between devices: 20.4 us -> 33.4 us  [through_mixing(): lax.all_to_all(apply_fn(lax.all_to_all(shaped, 'chan', split_axis=2, conc...]
    all_gather x1 -> x0, blocking collectives: 12.4 us -> none  [on_device(): lax.all_gather(generator.astype(jnp.bfloat16), 'blk', axis=1, tiled=True)]
    all_to_all x0 -> x1, waiting for transfers between devices: none -> 8.45 us  [search_the_spans(): lax.all_to_all(w_next, axis_name=mesh_ax, split_axis=0, concat_axis=0)]
    all_to_all x0 -> x1, starting transfers between devices: none -> 4.31 us  [search_the_spans(): lax.all_to_all(w_next, axis_name=mesh_ax, split_axis=0, concat_axis=0)]
  transfers between devices with their start and end apart: 4 -> 5, of which waited for: 3 -> 4; matrix products, arithmetic and copies ran while one was open for 4% -> 5% of each run, Pallas kernels for 0% -> 0%
where the time goes in v1:
time: 386 us; the launch traced here: 385 us
  blocking collectives  195 us (51%)
  waiting for transfers between devices  85.6 us (22%)
  local copies, waits for them, and re-layouts  45.4 us (12%)
  starting transfers between devices  40.9 us (11%)
  other arithmetic  8.61 us (2%)
  matrix products  8.37 us (2%)
    all_to_all x2, blocking collectives, through_mixing(): lax.all_to_all(shaped, 'chan', split_axis=2, concat_axis=1, tiled=True)  89.8 us
    all_gather x4, blocking collectives, commutator(): lax.all_gather(right_rows.astype(jnp.bfloat16), 'blk', axis=1, tiled=True)  54 us
    all_to_all x1, blocking collectives, through_mixing(): lax.all_to_all(apply_fn(lax.all_to_all(shaped, 'chan', split_axis=2, conc...  50.7 us
    all_to_all x1, waiting for transfers between devices, through_mixing(): lax.all_to_all(shaped, 'chan', split_axis=2, concat_axis=1, tiled=True)  43.8 us
    all_to_all x2, waiting for transfers between devices, through_mixing(): lax.all_to_all(apply_fn(lax.all_to_all(shaped, 'chan', split_axis=2, conc...  33.4 us
    all_to_all x1, starting transfers between devices, through_mixing(): lax.all_to_all(shaped, 'chan', split_axis=2, concat_axis=1, tiled=True)  19.4 us
    all_to_all x2, starting transfers between devices, through_mixing(): lax.all_to_all(apply_fn(lax.all_to_all(shaped, 'chan', split_axis=2, conc...  13.5 us
    all_to_all x1, waiting for transfers between devices, search_the_spans(): lax.all_to_all(w_next, axis_name=mesh_ax, split_axis=0, concat_axis=0)  8.45 us
  transfers between devices with their start and end apart: 5, of which 4 were waited for; matrix products, arithmetic and copies ran while one was open for 5% of the time, Pallas kernels for 0%

profile of v1, /device:TPU:33, one launch (start us, length us, event | category | flops | bytes accessed | tf_op | source)
XLA Modules:
  0.0 384.7 jit_solution(16500995667496572938)
XLA Ops:
  0.8 1.2 fusion.19
  2.2 2.2 gather_fusion.1
  5.2 2.2 gather_fusion.2
  8.1 1.5 copy.68
  9.6 19.4 %all-to-all-start.1 = ((f32[2,1,128,648]{3,0,1,2:T(2,128)}), f32[2,1,128,648]{3,0,1,2:T(2,128)S(1)}, u32[]{:S(2)}, u32[]{:S(2)}) async-start(f32[2,1,128,648]{3,0,1,2:T(2,128)} %copy.68), calls=%async_computation.1 | async-start | bytes 1572864 | tf_op jit(solution)/shard_map/all_to_all | solution.py:65
  29.0 0.8 fusion.23
  29.8 43.8 %all-to-all-done.1 = f32[2,1,128,648]{3,0,1,2:T(2,128)S(1)} async-done(((f32[2,1,128,648]{3,0,1,2:T(2,128)}), f32[2,1,128,648]{3,0,1,2:T(2,128)S(1)}, u32[]{:S(2)}, u32[]{:S(2)}) %all-to-all-start.1) | async-done | bytes 663584 | tf_op jit(solution)/shard_map/all_to_all | solution.py:65
  73.6 1.0 stack.34
  74.6 4.3 %all-to-all-start = ((bf16[4,1,144,576]{3,2,1,0:T(8,128)(2,1)}), bf16[4,1,144,576]{3,2,1,0:T(8,128)(2,1)S(1)}, u32[]{:S(2)}, u32[]{:S(2)}) async-start(bf16[4,1,144,576]{3,2,1,0:T(8,128)(2,1)} %stack.34), calls=%async_computation | async-start | bytes 1474560 | tf_op jit(solution)/shard_map/all_to_all | solution.py:12
  80.7 1.3 copy.70
  82.0 8.5 %all-to-all-done = bf16[4,1,144,576]{3,2,1,0:T(8,128)(2,1)S(1)} async-done(((bf16[4,1,144,576]{3,2,1,0:T(8,128)(2,1)}), bf16[4,1,144,576]{3,2,1,0:T(8,128)(2,1)S(1)}, u32[]{:S(2)}, u32[]{:S(2)}) %all-to-all-start) | async-done | bytes 663584 | tf_op jit(solution)/shard_map/all_to_all | solution.py:12
  90.5 7.3 %all-to-all-start.2 = ((f32[2,128,1,648]{3,0,2,1:T(2,128)}), f32[2,128,1,648]{3,0,2,1:T(2,128)}, u32[]{:S(2)}, u32[]{:S(2)}) async-start(f32[2,128,1,648]{3,0,2,1:T(2,128)} %copy.70), calls=%async_computation.2 | async-start | bytes 1572864 | tf_op jit(solution)/shard_map/all_to_all | solution.py:64
  99.5 11.9 %all_gather.12 = bf16[1,576,576]{2,1,0:T(8,128)(2,1)S(1)} all-gather(bf16[1,144,576]{2,1,0:T(8,128)(2,1)S(1)} %copy-done.10), channel_id=1, replica_groups=mesh['chan'=128,'blk'=4] {'blk'}, dimensions={1}, use_global_device_ids=true | all-gather | bytes 829440 | tf_op jit(solution)/shard_map/all_gather | solution.py:53
  112.4 2.2 gather_fusion
  114.8 1.1 stack.35
  115.9 26.2 %all-to-all-done.2 = f32[2,128,1,648]{3,0,2,1:T(2,128)} async-done(((f32[2,128,1,648]{3,0,2,1:T(2,128)}), f32[2,128,1,648]{3,0,2,1:T(2,128)}, u32[]{:S(2)}, u32[]{:S(2)}) %all-to-all-start.2) | async-done | bytes 663584 | tf_op jit(solution)/shard_map/all_to_all | solution.py:64
  142.1 2.1 fusion.43
  144.2 1.1 convert_element_type.107
  145.3 0.7 copy.97
  146.1 1.4 convert_element_type.103
  147.4 1.1 convert_element_type.101
  149.0 0.9 broadcast_in_dim.7
  149.9 3.6 all-to-all-start.3
  153.6 18.9 %all_gather.13 = bf16[1,576,576]{2,1,0:T(8,128)(2,1)S(1)} all-gather(bf16[1,144,576]{2,1,0:T(8,128)(2,1)S(1)} %copy-done.13), channel_id=1, replica_groups=mesh['chan'=128,'blk'=4] {'blk'}, dimensions={1}, use_global_device_ids=true | all-gather | bytes 829440 | tf_op jit(solution)/shard_map/all_gather | solution.py:53
  173.4 1.1 fusion.1
  174.5 1.4 stack.39
  176.0 0.8 copy.73
  176.8 52.9 %all_to_all.64 = f32[2,1,128,648]{3,1,0,2:T(1,128)S(1)} all-to-all(f32[2,1,128,648]{3,1,0,2:T(1,128)S(1)} %copy.73), channel_id=1, replica_groups=mesh['chan'=128,'blk'=4] {'chan'}, dimensions={2} | all-to-all | bytes 1327104 | tf_op jit(solution)/shard_map/all_to_all | solution.py:65
  230.2 1.0 copy.88
  233.5 0.9 pad_maximum_fusion.2
  234.4 2.3 copy.76
  236.7 50.7 %all_to_all.65 = f32[2,128,1,648]{3,2,0,1:T(1,128)S(1)} all-to-all(f32[2,128,1,648]{3,2,0,1:T(1,128)S(1)} %copy.76), channel_id=1, replica_groups=mesh['chan'=128,'blk'=4] {'chan'}, dimensions={1} | all-to-all | bytes 1327104 | tf_op jit(solution)/shard_map/all_to_all | solution.py:64
  287.4 1.3 fusion.41
  288.8 1.1 convert_element_type.112
  290.4 11.6 %all_gather.15 = bf16[1,576,576]{2,1,0:T(8,128)(2,1)S(1)} all-gather(bf16[1,144,576]{2,1,0:T(8,128)(2,1)S(1)} %convert_element_type.114), channel_id=1, replica_groups=mesh['chan'=128,'blk'=4] {'blk'}, dimensions={1}, use_global_device_ids=true | all-gather | bytes 829440 | tf_op jit(solution)/shard_map/all_gather | solution.py:53
  303.3 0.7 reshape_broadcast_in_dim.4
  304.0 36.9 %all_to_all.66 = f32[1,1,128,648]{3,1,0,2:T(1,128)S(1)} all-to-all(f32[1,1,128,648]{3,1,0,2:T(1,128)S(1)} %reshape_broadcast_in_dim.4), channel_id=1, replica_groups=mesh['chan'=128,'blk'=4] {'chan'}, dimensions={2} | all-to-all | bytes 663552 | tf_op jit(solution)/shard_map/all_to_all | solution.py:65
  342.2 1.2 copy.82
  343.5 6.2 %all-to-all-start.7 = ((f32[1,128,1,648]{3,2,0,1:T(1,128)}), f32[1,128,1,648]{3,2,0,1:T(1,128)S(1)}, u32[]{:S(2)}, u32[]{:S(2)}) async-start(f32[1,128,1,648]{3,2,0,1:T(1,128)} %copy.82), calls=%async_computation.7 | async-start | bytes 786432 | tf_op jit(solution)/shard_map/all_to_all | solution.py:64
  350.4 4.4 %sort.17 = (s32[576]{0:T(1024)}, s32[576]{0:T(1024)S(1)}) sort(s32[576]{0:T(1024)S(1)} %copy-done.19, s32[576]{0:T(1024)S(1)} %iota.20), dimensions={0}, to_apply=%region_0.0 | sort | flops 5760 | bytes 9216 | tf_op jit(solution)/shard_map/jit(argsort)/sort | solution.py:87
  355.4 2.2 gather_fusion.3
  357.8 11.7 %all-gather = bf16[576,576]{1,0:T(8,128)(2,1)S(1)} all-gather(bf16[144,576]{1,0:T(8,128)(2,1)S(1)} %fusion.32), channel_id=2, replica_groups=mesh['chan'=128,'blk'=4] {'blk'}, dimensions={0}, use_global_device_ids=true | all-gather | bytes 829440 | tf_op jit(solution)/shard_map/all_gather | solution.py:53
  369.5 1.2 fusion.38
  370.6 7.2 %all-to-all-done.7 = f32[1,128,1,648]{3,2,0,1:T(1,128)S(1)} async-done(((f32[1,128,1,648]{3,2,0,1:T(1,128)}), f32[1,128,1,648]{3,2,0,1:T(1,128)S(1)}, u32[]{:S(2)}, u32[]{:S(2)}) %all-to-all-start.7) | async-done | bytes 331808 | tf_op jit(solution)/shard_map/all_to_all | solution.py:64
  377.8 0.9 reduce.3
  379.4 2.8 gather_fusion.4
  382.2 1.3 copy.84
  383.6 1.1 fusion.8
  (97 shorter events, 15.8 us)
Async XLA Ops:
  0.0 78.9 %copy-start = (f32[128,128]{1,0:T(8,128)S(1)}, f32[128,128]{1,0:T(8,128)}, u32[]{:S(2)}) copy-start(f32[128,128]{1,0:T(8,128)} %param.16) | copy-start | bytes 196612
  0.0 0.7 copy-start.18
  0.7 111.0 %copy-start.14 = (pred[576]{0:T(1024)(128)(4,1)}, pred[576]{0:T(1024)(128)(4,1)S(1)}, u32[]{:S(2)}) copy-start(pred[576]{0:T(1024)(128)(4,1)S(1)} %iota_compare_fusion.3) | copy-start | bytes 1732
  0.8 111.0 %copy-start.16 = (pred[144]{0:T(512)(128)(4,1)}, pred[144]{0:T(512)(128)(4,1)S(1)}, u32[]{:S(2)}) copy-start(pred[144]{0:T(512)(128)(4,1)S(1)} %add_compare_fusion) | copy-start | bytes 436
  9.5 19.5 %copy-start.1 = (f32[1,144,576]{2,1,0:T(8,128)S(1)}, f32[1,144,576]{2,1,0:T(8,128)}, u32[]{:S(2)}) copy-start(f32[1,144,576]{2,1,0:T(8,128)} %param.10) | copy-start | bytes 995332
  9.6 19.5 %copy-start.2 = (f32[1,144,576]{2,1,0:T(8,128)S(1)}, f32[1,144,576]{2,1,0:T(8,128)}, u32[]{:S(2)}) copy-start(f32[1,144,576]{2,1,0:T(8,128)} %param.9) | copy-start | bytes 995332
  9.6 64.0 %all-to-all-start.1 = ((f32[2,1,128,648]{3,0,1,2:T(2,128)}), f32[2,1,128,648]{3,0,1,2:T(2,128)S(1)}, u32[]{:S(2)}, u32[]{:S(2)}) async-start(f32[2,1,128,648]{3,0,1,2:T(2,128)} %copy.68), calls=%async_computation.1 | async-start | bytes 1572864 | tf_op jit(solution)/shard_map/all_to_all | solution.py:65
  74.6 4.3 %copy-start.22 = (s32[128]{0:T(128)S(1)}, s32[128]{0:T(128)}, u32[]{:S(2)}) copy-start(s32[128]{0:T(128)} %param.14) | copy-start | bytes 1540
  74.6 4.6 %copy-start.23 = (s32[128]{0:T(128)S(1)}, s32[128]{0:T(128)}, u32[]{:S(2)}) copy-start(s32[128]{0:T(128)} %param.15) | copy-start | bytes 1540
  74.6 15.9 %all-to-all-start = ((bf16[4,1,144,576]{3,2,1,0:T(8,128)(2,1)}), bf16[4,1,144,576]{3,2,1,0:T(8,128)(2,1)S(1)}, u32[]{:S(2)}, u32[]{:S(2)}) async-start(bf16[4,1,144,576]{3,2,1,0:T(8,128)(2,1)} %stack.34), calls=%async_computation | async-start | bytes 1474560 | tf_op jit(solution)/shard_map/all_to_all | solution.py:12
  82.0 15.7 %copy-start.20 = (f32[1,576]{1,0:T(1,128)S(1)}, f32[1,576]{1,0:T(1,128)}, u32[]{:S(2)}) copy-start(f32[1,576]{1,0:T(1,128)} %param.11) | copy-start | bytes 6916
  90.5 51.6 %all-to-all-start.2 = ((f32[2,128,1,648]{3,0,2,1:T(2,128)}), f32[2,128,1,648]{3,0,2,1:T(2,128)}, u32[]{:S(2)}, u32[]{:S(2)}) async-start(f32[2,128,1,648]{3,0,2,1:T(2,128)} %copy.70), calls=%async_computation.2 | async-start | bytes 1572864 | tf_op jit(solution)/shard_map/all_to_all | solution.py:64
  97.8 0.7 copy-start.21
  98.5 0.9 copy-start.10
  98.9 47.1 %copy-start.3 = (f32[1,128,1,648]{3,1,2,0:T(8,128)}, f32[1,128,1,648]{3,1,2,0:T(8,128)S(1)}, u32[]{:S(2)}) copy-start(f32[1,128,1,648]{3,1,2,0:T(8,128)S(1)} %mul.105) | copy-start | bytes 995332
  149.0 23.5 %copy-start.5 = (bf16[144,576]{1,0:T(8,128)(2,1)}, bf16[144,576]{1,0:T(8,128)(2,1)S(1)}, u32[]{:S(2)}) copy-start(bf16[144,576]{1,0:T(8,128)(2,1)S(1)} %convert_element_type.105) | copy-start | bytes 497668
  149.9 3.6 copy-start.13
  149.9 22.9 %all-to-all-start.3 = ((bf16[4,1,144,576]{3,2,1,0:T(8,128)(2,1)}), bf16[4,1,144,576]{3,2,1,0:T(8,128)(2,1)S(1)}, u32[]{:S(2)}, u32[]{:S(2)}) async-start(bf16[4,1,144,576]{3,2,1,0:T(8,128)(2,1)} %broadcast_in_dim.7), calls=%async_computation.3 | async-start | bytes 1474560 | tf_op jit(solution)/shard_map/all_to_all | solution.py:28
  172.5 0.9 copy-start.11
  174.5 1.4 copy-start.7
  231.8 1.0 copy-start.9
  287.4 1.3 copy-start.4
  290.4 11.6 %copy-start.6 = (bf16[144,576]{1,0:T(8,128)(2,1)S(1)}, bf16[144,576]{1,0:T(8,128)(2,1)}, u32[]{:S(2)}) copy-start(bf16[144,576]{1,0:T(8,128)(2,1)} %copy-done.5) | copy-start | bytes 497668
  302.0 0.9 copy-start.12
  343.5 34.4 %all-to-all-start.7 = ((f32[1,128,1,648]{3,2,0,1:T(1,128)}), f32[1,128,1,648]{3,2,0,1:T(1,128)S(1)}, u32[]{:S(2)}, u32[]{:S(2)}) async-start(f32[1,128,1,648]{3,2,0,1:T(1,128)} %copy.82), calls=%async_computation.7 | async-start | bytes 786432 | tf_op jit(solution)/shard_map/all_to_all | solution.py:64
  349.7 0.7 copy-start.19
  357.8 11.7 %copy-start.15 = (pred[576]{0:T(1024)(128)(4,1)S(1)}, pred[576]{0:T(1024)(128)(4,1)}, u32[]{:S(2)}) copy-start(pred[576]{0:T(1024)(128)(4,1)} %copy-done.14) | copy-start | bytes 1732
  357.8 11.7 %copy-start.17 = (pred[144]{0:T(512)(128)(4,1)S(1)}, pred[144]{0:T(512)(128)(4,1)}, u32[]{:S(2)}) copy-start(pred[144]{0:T(512)(128)(4,1)} %copy-done.16) | copy-start | bytes 436
  382.2 1.3 copy-start.8
